TPU v7x, 512 devices: a whole 4x8x8 slice. The times are simulated.
512 devices in a mesh: ens: 8 (over y), grid: 64 (over x, z, core).
Axes of the slice: x: 4, y: 8, z: 8, core: 2. Of those that a mesh axis runs over, the one named last changes fastest.
Arguments:
- hidden: bfloat16 [8, 65536, 1024], P('ens', 'grid'), may hold values from -6 to 6
- weight: bfloat16 [1024, 100], replicated, may hold values from -0.1875 to 0.1875
- target: float32 [100, 65536], P(None, 'grid'), may hold values from -6 to 6
- area_weight: float32 [65536], P('grid'), may hold values from 0.3 to 3
- var_weight: float32 [100], replicated, may hold values from 0.25 to 4
- edge_owner: int32 [65536, 3], P('grid'), may hold values from 0 to 63, all different within a row; in each aligned block of 1024 rows (0 to 1023, 1024 to 2047, ...) at most 60 rows name the same one
- edge_row: int32 [65536, 3], P('grid'), may hold values from 0 to 127
- edge_weight: float32 [65536, 3], P('grid'), may hold values from 0.05 to 1
Outputs:
- grad_weight: float32 [1024, 100], P('grid')
- latent_gradient: bfloat16 [8, 8192, 1024], P('ens', 'grid')
Inputs may be any that keep to these rules, and one draw needn't show every extreme that they name: `edge_owner`: the 3 owners of one grid point differ; among the edges of the 1024 points of one device no owner appears more than 60 times, and some owner appears exactly 60 times.
All inputs are finite; a program needn't handle non-finite values.
Results may differ from a plain program's by a relative error of at most 0.0163.
Values may be sent and summed in bfloat16 or wider, within the bound.
A program may use at most 64 MiB of HBM per device.

v0:
```python
import functools
import math

import jax
import jax.numpy as jnp
from jax import lax
from jax.experimental import pallas as pl
from jax.experimental.pallas import tpu as pltpu
from jax.sharding import PartitionSpec as P

smooth_width = 0.1
LANES = 128
STEPS = 32000.0
VMEM_LIMIT = 62 * 1024 * 1024


def softened_sign(difference):
    return difference * lax.rsqrt(difference * difference + smooth_width * smooth_width)


def round_up(n, m):
    return (n + m - 1) // m * m


def score_block(x, t, scale):
    n = len(x)
    total = [None] * n
    for i in range(n):
        for j in range(i + 1, n):
            a = softened_sign(x[i] - x[j])
            total[i] = a if total[i] is None else total[i] + a
            total[j] = -a if total[j] is None else total[j] - a
    out = []
    for i in range(n):
        raw = softened_sign(x[i] - t) * (1.0 / n) - total[i] * (1.0 / (n * (n - 1)))
        out.append((scale * raw).astype(jnp.bfloat16))
    return out


def grid_shape(owners):
    return (owners // 16, 8, 2) if owners >= 16 else (owners // 4, 2, 2)


def place_slots(own_ref, row_ref, ew_ref, slot_s, w_s, r_s):
    owners, points = slot_s.shape
    neigh = own_ref.shape[0]
    tri = (
        lax.broadcasted_iota(jnp.int32, (LANES, LANES), 0)
        <= lax.broadcasted_iota(jnp.int32, (LANES, LANES), 1)
    ).astype(jnp.float32).astype(jnp.bfloat16)
    nx, nz, nc = grid_shape(owners)
    at = lax.broadcasted_iota(jnp.int32, (owners, LANES), 0)
    z_id = lax.shift_right_logical(at, int(math.log2(nx * nc)))
    x_id = jnp.bitwise_and(lax.shift_right_logical(at, int(math.log2(nc))), nx - 1)
    owner_id = (x_id * nz + z_id) * nc + jnp.bitwise_and(at, nc - 1)
    carry = jnp.zeros((owners, 1), jnp.float32)
    for b in range(0, points, LANES):
        hit = jnp.zeros((owners, LANES), jnp.float32)
        w = jnp.zeros((owners, LANES), jnp.float32)
        row = jnp.zeros((owners, LANES), jnp.float32)
        for k in range(neigh):
            same = own_ref[k : k + 1, b : b + LANES] == owner_id
            hit = jnp.where(same, 1.0, hit)
            w = jnp.where(same, ew_ref[k : k + 1, b : b + LANES], w)
            row = jnp.where(same, row_ref[k : k + 1, b : b + LANES].astype(jnp.float32), row)
        count = carry + jnp.dot(hit.astype(jnp.bfloat16), tri, preferred_element_type=jnp.float32)
        slot_s[:, b : b + LANES] = jnp.where(hit > 0.0, count, 0.0)
        w_s[:, b : b + LANES] = w
        r_s[:, b : b + LANES] = row
        carry = count[:, LANES - 1 : LANES]


def far_first(n):
    return sorted(range(n), key=lambda o: -min(o, n - o))


def bulk_wait(ref, sem):
    pltpu.make_async_copy(ref, ref, sem).wait()


def fused_kernel(
    cfg,
    hidden_hbm, wt_hbm, target_hbm, area_hbm, var_hbm, own_hbm, row_hbm, ew_hbm,
    gw_out, mesh_out,
    hid, wt_raw, target, area, var, own, row, ew,
    wt, w_col, x_send, x_recv, unit_s, g_send, g_recv,
    slot_s, w_s, r_s, a_s, wb_s, gt_s, out_buf, in_buf,
    d_send, d_recv, gw_s, half_s, half_recv, y_send, y_recv, q_s, q_recv, p_send, p_recv, r_send, r_recv,
    in_sem, x_ss, x_rs, g_ss, g_rs, m_ss, m_rs, d_ss, d_rs, h_ss, h_rs, y_ss, y_rs, q_ss, q_rs, p_ss, p_rs, r_ss, r_rs,
):
    variables, slots, share, normalizer = cfg
    members, grows, slab = g_send.shape
    owners, points = slot_s.shape
    latent = hid.shape[1]
    mesh_rows = d_send.shape[1]
    e, g = lax.axis_index("ens"), lax.axis_index("grid")
    nx, nz, nc = grid_shape(owners)
    nu = nx * nc
    z, core = lax.rem(g // nc, nz), lax.rem(g, nc)
    x_at = g // (nz * nc)
    u = x_at * nc + core

    def plane_peer(i):
        return ((i // nc) * nz + z) * nc + lax.rem(i, nc)

    def column_peer(i):
        return ((u // nc) * nz + i) * nc + lax.rem(u, nc)

    def send(src, dst, ss, rs, axis, peer, me):
        @pl.when(peer != me)
        def _():
            pltpu.make_async_remote_copy(
                src_ref=src, dst_ref=dst, send_sem=ss, recv_sem=rs,
                device_id={axis: peer}, device_id_type=pl.DeviceIdType.MESH,
            ).start()

        @pl.when(peer == me)
        def _():
            pltpu.make_async_copy(src, dst, rs).start()

    barrier = pltpu.get_barrier_semaphore()

    def greet_ens(i, _):
        pl.semaphore_signal(barrier, inc=1, device_id={"ens": lax.rem(e + i, members)}, device_id_type=pl.DeviceIdType.MESH)
        return 0

    def greet_plane(i, _):
        pl.semaphore_signal(barrier, inc=1, device_id={"grid": plane_peer(lax.rem(u + i, nu))}, device_id_type=pl.DeviceIdType.MESH)
        return 0

    def greet_column(i, _):
        pl.semaphore_signal(barrier, inc=1, device_id={"grid": column_peer(lax.rem(z + i, nz))}, device_id_type=pl.DeviceIdType.MESH)
        return 0

    chunk = 2 * slab
    loads = [pltpu.make_async_copy(wt_hbm, wt_raw, in_sem.at[0])]
    chunks = points // chunk
    order = [lax.rem(e // 2 + o, chunks) for o in far_first(chunks)]
    for c in order:
        rows = pl.ds(pl.multiple_of(c * chunk, chunk), chunk)
        loads.append(pltpu.make_async_copy(hidden_hbm.at[rows], hid.at[rows], in_sem.at[1 + c]))
    n_hid = len(loads)
    loads.append(
        pltpu.make_async_copy(
            target_hbm.at[:, pl.ds(pl.multiple_of(e * slab, slab), slab)], target, in_sem.at[n_hid]
        )
    )
    for i, (s, d) in enumerate(((area_hbm, area), (var_hbm, var), (own_hbm, own), (row_hbm, row), (ew_hbm, ew))):
        loads.append(pltpu.make_async_copy(s, d, in_sem.at[n_hid + 1 + i]))
    for cp in loads:
        cp.start()
    lax.fori_loop(1, members, greet_ens, 0)
    lax.fori_loop(1, nu, greet_plane, 0)
    lax.fori_loop(1, nz, greet_column, 0)

    loads[0].wait()
    whole = variables // 16 * 16
    wt[0:whole, :] = wt_raw[0:whole, :]
    wt[whole : whole + 16, :] = jnp.concatenate(
        [wt_raw[whole:variables, :], jnp.zeros((whole + 16 - variables, latent), jnp.bfloat16)], axis=0
    )
    wt[whole + 16 :, :] = jnp.zeros((LANES - whole - 16, latent), jnp.bfloat16)
    for b in range(0, latent, LANES):
        w_col[b : b + LANES, :] = wt[:, b : b + LANES].astype(jnp.float32).T.astype(jnp.bfloat16)

    tail_row = lax.broadcasted_iota(jnp.int32, (8, slab), 0)
    zero_rows = jnp.zeros((8, slab), jnp.int32)
    for t, c in enumerate(order):
        loads[1 + t].wait()
        rows = pl.ds(pl.multiple_of(c * chunk, chunk), chunk)
        part = jnp.dot(hid[rows, :], w_col[...], preferred_element_type=jnp.float32)
        for s in range(2):
            m = 2 * c + s
            block = part[s * slab : (s + 1) * slab, :].T[: whole + 8, :]
            top = jnp.max(jnp.abs(block), axis=0, keepdims=True)
            power = jnp.ceil(jnp.log2(jnp.maximum(top, 1e-30)))
            code = jnp.floor(block * (jnp.exp2(-power) * STEPS) + 0.5).astype(jnp.int32)
            tail = jnp.where(tail_row == variables - whole, power.astype(jnp.int32), code[whole:, :])
            x_send[m, 0:whole, :] = code[0:whole, :].astype(jnp.int16)
            x_send[m, whole : whole + 16, :] = jnp.concatenate([tail, zero_rows], axis=0).astype(jnp.int16)
        if t == 0:
            pl.semaphore_wait(barrier, members + nu + nz - 3)
        for s in range(2):
            m = 2 * c + s
            send(x_send.at[m], x_recv.at[e], x_ss, x_rs, "ens", m, e)

    for cp in loads[n_hid:]:
        cp.wait()
    place_slots(own, row, ew, slot_s, w_s, r_s)
    want = lax.broadcasted_iota(jnp.int32, (slots, points), 0).astype(jnp.float32) + 1.0
    lane = lax.broadcasted_iota(jnp.int32, (slots, LANES), 1)

    def one_hot(o, _):
        same = slot_s[pl.ds(o, 1), :] == want
        at = pl.ds(pl.multiple_of(o * slots, slots), slots)
        a_s[at, :] = jnp.where(same, 1.0, 0.0).astype(jnp.bfloat16)
        w = jnp.sum(jnp.where(same, w_s[pl.ds(o, 1), :], 0.0), axis=1, keepdims=True)
        r = jnp.sum(jnp.where(same, r_s[pl.ds(o, 1), :], 0.0), axis=1, keepdims=True)
        wb_s[at, :] = jnp.where(lane == variables, r, w)
        return 0

    lax.fori_loop(0, owners, one_hot, 0)
    vcol = jnp.broadcast_to(
        jnp.concatenate([var[...], jnp.zeros((1, LANES - variables), jnp.float32)], axis=1), (LANES, LANES)
    ).T
    scale = vcol * area[pl.ds(e, 1), :]
    q_s[0:LANES, :] = scale

    bulk_wait(x_recv, x_rs)

    def wide_block(m, at):
        return x_recv[m, at, :].astype(jnp.int32).astype(jnp.float32)

    for m in range(members):
        power = wide_block(m, pl.ds(whole, 16))[variables - whole : variables - whole + 1, :]
        unit_s[m] = jnp.broadcast_to(jnp.exp2(power) * (1.0 / STEPS), (16, slab))

    def score(r, t):
        at = pl.ds(r, 16)
        got = score_block([wide_block(m, at) * unit_s[m] for m in range(members)], t, q_s[at, :])
        for m in range(members):
            g_send[m, at, :] = got[m]

    def score_step(i, _):
        r = pl.multiple_of(i * 16, 16)
        score(r, target[pl.ds(r, 16), :])
        return 0

    lax.fori_loop(0, variables // 16, score_step, 0)
    score(
        whole,
        jnp.concatenate(
            [target[whole:variables, :], jnp.zeros((whole + 16 - variables, slab), jnp.float32)], axis=0
        ),
    )
    for o in far_first(members):
        m = lax.rem(e + o, members)
        send(g_send.at[m], g_recv.at[e], g_ss, g_rs, "ens", m, e)

    bulk_wait(g_recv, g_rs)
    pad = jnp.zeros((LANES - grows, LANES), jnp.float32)
    lane = lax.broadcasted_iota(jnp.int32, (LANES, LANES), 1)
    for s in range(members):
        block = jnp.concatenate([g_recv[s].astype(jnp.float32), pad], axis=0).T
        gt_s[s * LANES : (s + 1) * LANES, :] = jnp.where(lane == variables, 1.0, block).astype(jnp.bfloat16)
    step = nu * slots
    both = min(2, nz)
    groups = nz // both

    def messages(t, _):
        at = lax.rem(z // both + 1 + t, groups)
        rows = pl.ds(pl.multiple_of(at * (both * step), both * step), both * step)
        picked = jnp.dot(a_s[rows, :], gt_s[...], preferred_element_type=jnp.float32)
        zs = pl.ds(at * both, both)
        out_buf[zs] = (picked * wb_s[rows, :]).astype(jnp.bfloat16).reshape(both, nu, slots, LANES)
        for o in far_first(nx):
            for c in range(nc):
                j = lax.rem(x_at + o, nx) * nc + lax.rem(core + 1 + c, nc)
                send(out_buf.at[zs, j], in_buf.at[zs, u], m_ss, m_rs.at[at], "grid", plane_peer(j), g)
        return 0

    lax.fori_loop(0, 1, messages, 0)

    wide = jnp.concatenate([g_recv[s] for s in range(members)], axis=1)
    for b in range(0, latent, 2 * LANES):
        part = jnp.dot(wide, hid[:, b : b + 2 * LANES], preferred_element_type=jnp.float32)
        for c in range(0, 2 * LANES, LANES):
            gw_s[b + c : b + c + LANES, :] = jnp.concatenate([part[:, c : c + LANES], pad], axis=0).T
    run = nz * share
    per_member = nx * run
    for c in range(nc):
        for m in range(members):
            for v in range(nx):
                for i in range(share):
                    first = (v * nz * nc + c) * members * share + share * m + i
                    half_s[c, pl.ds(m * per_member + v * run + i, nz, share), :] = gw_s[
                        pl.ds(first, nz, nc * members * share), :
                    ]
    half = pltpu.make_async_remote_copy(
        src_ref=half_s.at[1 - core], dst_ref=half_recv, send_sem=h_ss, recv_sem=h_rs,
        device_id={"grid": g + 1 - 2 * core}, device_id_type=pl.DeviceIdType.MESH,
    )
    half.start()

    lax.fori_loop(1, max(1, groups // 2), messages, 0)

    half.wait_recv()
    for m in range(members):
        rows = pl.ds(m * per_member, per_member)
        y_send[m] = half_s[core, rows, :] + half_recv[rows, :]
    for o in far_first(members):
        m = lax.rem(e + o, members)
        send(y_send.at[m], y_recv.at[e], y_ss, y_rs, "ens", m, e)

    lax.fori_loop(max(1, groups // 2), groups, messages, 0)

    pick = (lax.broadcasted_iota(jnp.int32, (16, LANES), 1) == variables).astype(jnp.float32).astype(jnp.bfloat16)
    ids = lax.broadcasted_iota(jnp.int32, (mesh_rows, step), 0).astype(jnp.float32)

    def mesh_part(t, _):
        at = lax.rem(z // both + 1 + t, groups)
        zs = pl.ds(at * both, both)
        bulk_wait(in_buf.at[zs], m_rs.at[at])
        for i in range(both):
            zi = at * both + i
            block = in_buf[zi].reshape(step, LANES)
            place = lax.dot_general(pick, block, (((1,), (1,)), ((), ())), preferred_element_type=jnp.float32)
            picker = jnp.where(place[0:1, :] == ids, 1.0, 0.0).astype(jnp.bfloat16)
            d_send[zi] = jnp.dot(picker, block, preferred_element_type=jnp.float32).astype(jnp.bfloat16)
            send(d_send.at[zi], d_recv.at[z], d_ss, d_rs, "grid", column_peer(zi), g)
        return 0

    lax.fori_loop(0, groups // 2, mesh_part, 0)

    bulk_wait(y_recv, y_rs)
    total = y_recv[0]
    for m in range(1, members):
        total = total + y_recv[m]
    q_s[0:per_member, :] = total
    for j in range(nx):
        send(q_s.at[pl.ds(j * run, run)], q_recv.at[x_at], q_ss, q_rs, "grid", plane_peer(j * nc + core), g)

    lax.fori_loop(groups // 2, groups - 1, mesh_part, 0)

    bulk_wait(q_recv, q_rs)
    total = q_recv[0]
    for j in range(1, nx):
        total = total + q_recv[j]
    for j in range(nz):
        p_send[j] = total[j * share : (j + 1) * share, :]
    for j in range(nz):
        send(p_send.at[j], p_recv.at[z], p_ss, p_rs, "grid", column_peer(j), g)

    lax.fori_loop(groups - 1, groups, mesh_part, 0)

    bulk_wait(p_recv, p_rs)
    r_send[...] = jnp.sum(p_recv[...], axis=0) * normalizer
    for m in range(members):
        send(r_send, r_recv.at[e], r_ss, r_rs, "ens", m, e)
    bulk_wait(d_recv, d_rs)
    acc = d_recv[0].astype(jnp.float32)
    for j in range(1, nz):
        acc = acc + d_recv[j].astype(jnp.float32)
    mesh_out[...] = acc.astype(jnp.bfloat16)
    bulk_wait(r_recv, r_rs)
    for m in range(members):
        gw_out[share * m : share * (m + 1), :] = r_recv[m]

    bulk_wait(x_send.at[pl.ds(0, members - 1)], x_ss)
    bulk_wait(g_send.at[pl.ds(0, members - 1)], g_ss)
    bulk_wait(out_buf.at[:, pl.ds(0, nu - 1)], m_ss)
    bulk_wait(d_send.at[pl.ds(0, nz - 1)], d_ss)
    half.wait_send()
    bulk_wait(y_send.at[pl.ds(0, members - 1)], y_ss)
    bulk_wait(q_recv.at[pl.ds(0, nx - 1)], q_ss)
    bulk_wait(p_send.at[pl.ds(0, nz - 1)], p_ss)
    bulk_wait(r_recv.at[pl.ds(0, members - 1)], r_ss)


def finish_kernel(gw_ref, mesh_ref, wt_ref, gw_out, mesh_out):
    variables, latent = wt_ref.shape
    gw_out[...] = gw_ref[:, 0:variables]
    whole = variables // 16 * 16
    wide = jnp.concatenate(
        [wt_ref[whole:variables, :], jnp.zeros((whole + 16 - variables, latent), jnp.bfloat16)], axis=0
    )
    total = jnp.dot(mesh_ref[:, 0:whole], wt_ref[0:whole, :], preferred_element_type=jnp.float32)
    total = total + jnp.dot(mesh_ref[:, whole : whole + 16], wide, preferred_element_type=jnp.float32)
    mesh_out[...] = total.astype(jnp.bfloat16)


def per_device(hidden, weight, target, area_weight, var_weight, edge_owner, edge_row, edge_weight):
    rows = hidden[0]
    points, latent = rows.shape
    variables = weight.shape[1]
    neigh = edge_owner.shape[1]
    members = lax.axis_size("ens")
    owners = lax.axis_size("grid")
    mesh_rows = points // 8
    slab = points // members
    assert slab == LANES and variables < LANES
    capacity = max(2, (5 * points * neigh + 4 * owners - 1) // (4 * owners))
    slots = round_up(capacity, 16)
    grows = round_up(variables, 16)
    assert variables % 16 in range(1, 8)
    nx, nz, nc = grid_shape(owners)
    nu = nx * nc
    share = latent // (owners * members)
    normalizer = 1.0 / math.sqrt(float(points * owners * members))
    f32, bf16, i32 = jnp.float32, jnp.bfloat16, jnp.int32
    hbm = pl.BlockSpec(memory_space=pltpu.HBM)
    vmem = pl.BlockSpec(memory_space=pltpu.VMEM)
    dma = pltpu.SemaphoreType.DMA
    wt = weight.T
    gw, mesh_sum = pl.pallas_call(
        functools.partial(fused_kernel, (variables, slots, share, normalizer)),
        in_specs=[hbm] * 8,
        out_specs=[vmem] * 2,
        out_shape=[
            jax.ShapeDtypeStruct((members * share, LANES), f32),
            jax.ShapeDtypeStruct((mesh_rows, LANES), bf16),
        ],
        scratch_shapes=[
            pltpu.VMEM((points, latent), bf16),
            pltpu.VMEM((variables, latent), bf16),
            pltpu.VMEM((variables, slab), f32),
            pltpu.VMEM((points // LANES, LANES), f32),
            pltpu.VMEM((1, variables), f32),
            pltpu.VMEM((neigh, points), i32),
            pltpu.VMEM((neigh, points), i32),
            pltpu.VMEM((neigh, points), f32),
            pltpu.VMEM((LANES, latent), bf16),
            pltpu.VMEM((latent, LANES), bf16),
            pltpu.VMEM((members, grows, slab), jnp.int16),
            pltpu.VMEM((members, grows, slab), jnp.int16),
            pltpu.VMEM((members, 16, slab), f32),
            pltpu.VMEM((members, grows, slab), bf16),
            pltpu.VMEM((members, grows, slab), bf16),
            pltpu.VMEM((owners, points), f32),
            pltpu.VMEM((owners, points), f32),
            pltpu.VMEM((owners, points), f32),
            pltpu.VMEM((owners * slots, points), bf16),
            pltpu.VMEM((owners * slots, LANES), f32),
            pltpu.VMEM((points, LANES), bf16),
            pltpu.VMEM((nz, nu, slots, LANES), bf16),
            pltpu.VMEM((nz, nu, slots, LANES), bf16),
            pltpu.VMEM((nz, mesh_rows, LANES), bf16),
            pltpu.VMEM((nz, mesh_rows, LANES), bf16),
            pltpu.VMEM((latent, LANES), f32),
            pltpu.VMEM((nc, latent // nc, LANES), f32),
            pltpu.VMEM((latent // nc, LANES), f32),
            pltpu.VMEM((members, nx * nz * share, LANES), f32),
            pltpu.VMEM((members, nx * nz * share, LANES), f32),
            pltpu.VMEM((max(LANES, owners * share), LANES), f32),
            pltpu.VMEM((nx, nz * share, LANES), f32),
            pltpu.VMEM((nz, share, LANES), f32),
            pltpu.VMEM((nz, share, LANES), f32),
            pltpu.VMEM((share, LANES), f32),
            pltpu.VMEM((members, share, LANES), f32),
            dma((7 + points // (2 * slab),)),
            dma(()), dma(()), dma(()), dma(()), dma(()), dma((nz,)), dma(()), dma(()),
            dma(()), dma(()), dma(()), dma(()), dma(()), dma(()), dma(()), dma(()), dma(()), dma(()),
        ],
        compiler_params=pltpu.CompilerParams(
            collective_id=0, has_side_effects=True, vmem_limit_bytes=VMEM_LIMIT
        ),
    )(
        rows, wt, target, area_weight.reshape(points // LANES, LANES), var_weight.reshape(1, variables),
        edge_owner.T, edge_row.T, edge_weight.T,
    )
    grad_weight, mesh_grad = pl.pallas_call(
        finish_kernel,
        in_specs=[vmem] * 3,
        out_specs=[vmem] * 2,
        out_shape=[
            jax.ShapeDtypeStruct((members * share, variables), f32),
            jax.ShapeDtypeStruct((mesh_rows, latent), bf16),
        ],
        compiler_params=pltpu.CompilerParams(vmem_limit_bytes=VMEM_LIMIT),
    )(gw, mesh_sum, wt)
    return grad_weight, mesh_grad[None]


def solution(mesh):
    return jax.shard_map(
        per_device,
        mesh=mesh,
        in_specs=(
            P("ens", "grid", None),
            P(),
            P(None, "grid"),
            P("grid"),
            P(),
            P("grid", None),
            P("grid", None),
            P("grid", None),
        ),
        out_specs=(P("grid", None), P("ens", "grid", None)),
        check_vma=False,
    )
```

profile of v0, /device:TPU:1, one launch (start us, length us, event | category | flops | bytes accessed | tf_op | source)
XLA Modules:
  0.0 61.7 jit_solution(10602488106704151738)
XLA Ops:
  0.6 59.1 %shard_map.95 = (f32[16,128]{1,0:T(8,128)}, bf16[128,128]{1,0:T(8,128)(2,1)}) custom-call(bf16[1024,1024]{1,0:T(8,128)(2,1)} %bitcast.8, bf16[100,1024]{1,0:T(8,128)(2,1)} %bitcast.9, f32[100,1024]{1,0:T(8,128)} %target_hbm.1, f32[8,128]{1,0:T(8,128)} %bitcast.14, f32[1,100]{1,0:T(1,128)} %bitcast.15, s32[3,1024]{1,0:T(4,128)} %bitcast.11, ...), custom_call_target="tpu_custom_call" | custom-call | tf_op jit(solution)/shard_map/pallas_call | solution.py:395
  59.7 2.0 %shard_map.96 = (f32[16,100]{1,0:T(8,128)}, bf16[128,1024]{1,0:T(8,128)(2,1)}) custom-call(f32[16,128]{1,0:T(8,128)} %get-tuple-element.6.gw_ref, bf16[128,128]{1,0:T(8,128)(2,1)} %get-tuple-element.7.mesh_ref, bf16[100,1024]{1,0:T(8,128)(2,1)} %bitcast.10), custom_call_target="tpu_custom_call" | custom-call | tf_op jit(solution)/shard_map/pallas_call | solution.py:451
where the time goes:
time: 62.5 us; the launch traced here: 61.7 us
  Pallas kernels  61.1 us (98%)
  between operations  0.64 us (1%)
    pallas_call x1, Pallas kernels, per_device(): pl.pallas_call(functools.partial(fused_kernel, (variables, slots, share,...  59.1 us
    pallas_call x1, Pallas kernels, per_device(): pl.pallas_call(finish_kernel, in_specs=[vmem] * 3, out_specs=[vmem] * 2,...  2.01 us

commit v1 on v0

--- a/solution.py
+++ b/solution.py
@@ -41,7 +41,7 @@
     return (owners // 16, 8, 2) if owners >= 16 else (owners // 4, 2, 2)
 
 
-def place_slots(own_ref, row_ref, ew_ref, slot_s, w_s, r_s):
+def place_slots(own_ref, row_ref, ew_ref, slot_s, x_s):
     owners, points = slot_s.shape
     neigh = own_ref.shape[0]
     tri = (
@@ -53,21 +53,28 @@
     z_id = lax.shift_right_logical(at, int(math.log2(nx * nc)))
     x_id = jnp.bitwise_and(lax.shift_right_logical(at, int(math.log2(nc))), nx - 1)
     owner_id = (x_id * nz + z_id) * nc + jnp.bitwise_and(at, nc - 1)
+    line = lax.broadcasted_iota(jnp.int32, (16, LANES), 0)
+    blank = jnp.zeros((LANES - 16, LANES), jnp.float32)
     carry = jnp.zeros((owners, 1), jnp.float32)
     for b in range(0, points, LANES):
         hit = jnp.zeros((owners, LANES), jnp.float32)
-        w = jnp.zeros((owners, LANES), jnp.float32)
-        row = jnp.zeros((owners, LANES), jnp.float32)
+        vals = jnp.zeros((16, LANES), jnp.float32)
+        owns = jnp.zeros((16, LANES), jnp.float32)
         for k in range(neigh):
-            same = own_ref[k : k + 1, b : b + LANES] == owner_id
-            hit = jnp.where(same, 1.0, hit)
-            w = jnp.where(same, ew_ref[k : k + 1, b : b + LANES], w)
-            row = jnp.where(same, row_ref[k : k + 1, b : b + LANES].astype(jnp.float32), row)
+            own = own_ref[k : k + 1, b : b + LANES]
+            hit = jnp.where(own == owner_id, 1.0, hit)
+            rest = ew_ref[k : k + 1, b : b + LANES]
+            for i in range(3):
+                piece = rest.astype(jnp.bfloat16).astype(jnp.float32)
+                vals = jnp.where(line == 4 * k + i, piece, vals)
+                rest = rest - piece
+            vals = jnp.where(line == 4 * k + 3, row_ref[k : k + 1, b : b + LANES].astype(jnp.float32), vals)
+            owns = jnp.where((line >= 4 * k) & (line < 4 * k + 4), own.astype(jnp.float32), owns)
         count = carry + jnp.dot(hit.astype(jnp.bfloat16), tri, preferred_element_type=jnp.float32)
         slot_s[:, b : b + LANES] = jnp.where(hit > 0.0, count, 0.0)
-        w_s[:, b : b + LANES] = w
-        r_s[:, b : b + LANES] = row
         carry = count[:, LANES - 1 : LANES]
+        x_s[b : b + LANES, 0:LANES] = jnp.concatenate([vals, blank], axis=0).T.astype(jnp.bfloat16)
+        x_s[b : b + LANES, LANES:] = jnp.concatenate([owns, blank], axis=0).T.astype(jnp.bfloat16)
 
 
 def far_first(n):
@@ -84,8 +91,8 @@
     gw_out, mesh_out,
     hid, wt_raw, target, area, var, own, row, ew,
     wt, w_col, x_send, x_recv, unit_s, g_send, g_recv,
-    slot_s, w_s, r_s, a_s, wb_s, gt_s, out_buf, in_buf,
-    d_send, d_recv, gw_s, half_s, half_recv, y_send, y_recv, q_s, q_recv, p_send, p_recv, r_send, r_recv,
+    slot_s, x_s, a_s, sel_s, wb_s, gt_s, out_buf, in_buf,
+    d_send, d_recv, gw_s, half_recv, y_send, y_recv, q_s, gq_s, q_recv, p_send, p_recv, r_send, r_recv,
     in_sem, x_ss, x_rs, g_ss, g_rs, m_ss, m_rs, d_ss, d_rs, h_ss, h_rs, y_ss, y_rs, q_ss, q_rs, p_ss, p_rs, r_ss, r_rs,
 ):
     variables, slots, share, normalizer = cfg
@@ -186,20 +193,37 @@
 
     for cp in loads[n_hid:]:
         cp.wait()
-    place_slots(own, row, ew, slot_s, w_s, r_s)
-    want = lax.broadcasted_iota(jnp.int32, (slots, points), 0).astype(jnp.float32) + 1.0
-    lane = lax.broadcasted_iota(jnp.int32, (slots, LANES), 1)
-
-    def one_hot(o, _):
-        same = slot_s[pl.ds(o, 1), :] == want
-        at = pl.ds(pl.multiple_of(o * slots, slots), slots)
-        a_s[at, :] = jnp.where(same, 1.0, 0.0).astype(jnp.bfloat16)
-        w = jnp.sum(jnp.where(same, w_s[pl.ds(o, 1), :], 0.0), axis=1, keepdims=True)
-        r = jnp.sum(jnp.where(same, r_s[pl.ds(o, 1), :], 0.0), axis=1, keepdims=True)
-        wb_s[at, :] = jnp.where(lane == variables, r, w)
-        return 0
-
-    lax.fori_loop(0, owners, one_hot, 0)
+    place_slots(own, row, ew, slot_s, x_s)
+    step = nu * slots
+    both = min(2, nz)
+    groups = nz // both
+    want = lax.broadcasted_iota(jnp.int32, (slots, LANES), 0).astype(jnp.float32) + 1.0
+    line = lax.broadcasted_iota(jnp.int32, (LANES, LANES), 0)
+    lane = lax.broadcasted_iota(jnp.int32, (LANES, LANES), 1)
+    spread = jnp.where((lax.rem(line, 4) == 3) == (lane == variables), 1.0, 0.0).astype(jnp.bfloat16)
+
+    def one_hot(t, _):
+        at = lax.rem(z // both + 1 + t, groups)
+        base = pl.multiple_of(at * (both * nu), both * nu)
+        slot_g = slot_s[pl.ds(base, both * nu), :]
+        first = at * (both * step)
+        for j in range(both * nu):
+            rows = pl.ds(pl.multiple_of(first + j * slots, slots), slots)
+            for b in range(0, points, LANES):
+                same = slot_g[j : j + 1, b : b + LANES] == want
+                a_s[rows, b : b + LANES] = jnp.where(same, 1.0, 0.0).astype(jnp.bfloat16)
+        rows = pl.ds(pl.multiple_of(first, both * step), both * step)
+        ext = jnp.dot(a_s[rows, :], x_s[...], preferred_element_type=jnp.float32)
+        for j in range(both * nu):
+            owner = (((j % nu) // nc) * nz + at * both + j // nu) * nc + j % nc
+            part = ext[j * slots : (j + 1) * slots, :]
+            mine = part[:, LANES:] == owner.astype(jnp.float32)
+            sel_s[j * slots : (j + 1) * slots, :] = jnp.where(mine, part[:, 0:LANES], 0.0).astype(jnp.bfloat16)
+        wb_s[rows, :] = jnp.dot(sel_s[...], spread, preferred_element_type=jnp.float32)
+        return 0
+
+    early = (groups + 1) // 2
+    lax.fori_loop(0, early, one_hot, 0)
     vcol = jnp.broadcast_to(
         jnp.concatenate([var[...], jnp.zeros((1, LANES - variables), jnp.float32)], axis=1), (LANES, LANES)
     ).T
@@ -237,16 +261,13 @@
         m = lax.rem(e + o, members)
         send(g_send.at[m], g_recv.at[e], g_ss, g_rs, "ens", m, e)
 
+    lax.fori_loop(early, groups, one_hot, 0)
+
     bulk_wait(g_recv, g_rs)
     pad = jnp.zeros((LANES - grows, LANES), jnp.float32)
-    lane = lax.broadcasted_iota(jnp.int32, (LANES, LANES), 1)
     for s in range(members):
         block = jnp.concatenate([g_recv[s].astype(jnp.float32), pad], axis=0).T
         gt_s[s * LANES : (s + 1) * LANES, :] = jnp.where(lane == variables, 1.0, block).astype(jnp.bfloat16)
-    step = nu * slots
-    both = min(2, nz)
-    groups = nz // both
-
     def messages(t, _):
         at = lax.rem(z // both + 1 + t, groups)
         rows = pl.ds(pl.multiple_of(at * (both * step), both * step), both * step)
@@ -265,19 +286,13 @@
     for b in range(0, latent, 2 * LANES):
         part = jnp.dot(wide, hid[:, b : b + 2 * LANES], preferred_element_type=jnp.float32)
         for c in range(0, 2 * LANES, LANES):
-            gw_s[b + c : b + c + LANES, :] = jnp.concatenate([part[:, c : c + LANES], pad], axis=0).T
-    run = nz * share
-    per_member = nx * run
-    for c in range(nc):
-        for m in range(members):
-            for v in range(nx):
-                for i in range(share):
-                    first = (v * nz * nc + c) * members * share + share * m + i
-                    half_s[c, pl.ds(m * per_member + v * run + i, nz, share), :] = gw_s[
-                        pl.ds(first, nz, nc * members * share), :
-                    ]
+            block = jnp.concatenate([part[:, c : c + LANES], pad], axis=0).T
+            pairs = LANES // (nc * members * share)
+            gw_s[(b + c) // LANES * pairs : ((b + c) // LANES + 1) * pairs] = block.reshape(
+                pairs, nc, members * share, LANES
+            )
     half = pltpu.make_async_remote_copy(
-        src_ref=half_s.at[1 - core], dst_ref=half_recv, send_sem=h_ss, recv_sem=h_rs,
+        src_ref=gw_s.at[:, 1 - core], dst_ref=half_recv, send_sem=h_ss, recv_sem=h_rs,
         device_id={"grid": g + 1 - 2 * core}, device_id_type=pl.DeviceIdType.MESH,
     )
     half.start()
@@ -285,9 +300,9 @@
     lax.fori_loop(1, max(1, groups // 2), messages, 0)
 
     half.wait_recv()
+    total = gw_s[:, core] + half_recv[...]
     for m in range(members):
-        rows = pl.ds(m * per_member, per_member)
-        y_send[m] = half_s[core, rows, :] + half_recv[rows, :]
+        y_send[m] = total[:, m * share : (m + 1) * share, :]
     for o in far_first(members):
         m = lax.rem(e + o, members)
         send(y_send.at[m], y_recv.at[e], y_ss, y_rs, "ens", m, e)
@@ -316,9 +331,9 @@
     total = y_recv[0]
     for m in range(1, members):
         total = total + y_recv[m]
-    q_s[0:per_member, :] = total
+    gq_s[...] = total.reshape(nx, nz, share, LANES)
     for j in range(nx):
-        send(q_s.at[pl.ds(j * run, run)], q_recv.at[x_at], q_ss, q_rs, "grid", plane_peer(j * nc + core), g)
+        send(gq_s.at[j], q_recv.at[x_at], q_ss, q_rs, "grid", plane_peer(j * nc + core), g)
 
     lax.fori_loop(groups // 2, groups - 1, mesh_part, 0)
 
@@ -326,8 +341,7 @@
     total = q_recv[0]
     for j in range(1, nx):
         total = total + q_recv[j]
-    for j in range(nz):
-        p_send[j] = total[j * share : (j + 1) * share, :]
+    p_send[...] = total
     for j in range(nz):
         send(p_send.at[j], p_recv.at[z], p_ss, p_rs, "grid", column_peer(j), g)
 
@@ -417,22 +431,22 @@
             pltpu.VMEM((members, grows, slab), bf16),
             pltpu.VMEM((members, grows, slab), bf16),
             pltpu.VMEM((owners, points), f32),
-            pltpu.VMEM((owners, points), f32),
-            pltpu.VMEM((owners, points), f32),
+            pltpu.VMEM((points, 2 * LANES), bf16),
             pltpu.VMEM((owners * slots, points), bf16),
+            pltpu.VMEM((min(2, nz) * nu * slots, LANES), bf16),
             pltpu.VMEM((owners * slots, LANES), f32),
             pltpu.VMEM((points, LANES), bf16),
             pltpu.VMEM((nz, nu, slots, LANES), bf16),
             pltpu.VMEM((nz, nu, slots, LANES), bf16),
             pltpu.VMEM((nz, mesh_rows, LANES), bf16),
             pltpu.VMEM((nz, mesh_rows, LANES), bf16),
-            pltpu.VMEM((latent, LANES), f32),
-            pltpu.VMEM((nc, latent // nc, LANES), f32),
-            pltpu.VMEM((latent // nc, LANES), f32),
-            pltpu.VMEM((members, nx * nz * share, LANES), f32),
-            pltpu.VMEM((members, nx * nz * share, LANES), f32),
-            pltpu.VMEM((max(LANES, owners * share), LANES), f32),
-            pltpu.VMEM((nx, nz * share, LANES), f32),
+            pltpu.VMEM((nx * nz, nc, members * share, LANES), f32),
+            pltpu.VMEM((nx * nz, members * share, LANES), f32),
+            pltpu.VMEM((members, nx * nz, share, LANES), f32),
+            pltpu.VMEM((members, nx * nz, share, LANES), f32),
+            pltpu.VMEM((LANES, LANES), f32),
+            pltpu.VMEM((nx, nz, share, LANES), f32),
+            pltpu.VMEM((nx, nz, share, LANES), f32),
             pltpu.VMEM((nz, share, LANES), f32),
             pltpu.VMEM((nz, share, LANES), f32),
             pltpu.VMEM((share, LANES), f32),

time: 62.5 us -> 56 us (0.90)
  Pallas kernels: 61.1 us -> 55.1 us
    pallas_call x1, Pallas kernels: 59.1 us -> 53 us  [per_device(): pl.pallas_call(functools.partial(fused_kernel, (variables, slots, share,...]
where the time goes in v1:
time: 56 us; the launch traced here: 55.7 us
  Pallas kernels  55.1 us (98%)
  between operations  0.64 us (1%)
    pallas_call x1, Pallas kernels, per_device(): pl.pallas_call(functools.partial(fused_kernel, (variables, slots, share,...  53 us
    pallas_call x1, Pallas kernels, per_device(): pl.pallas_call(finish_kernel, in_specs=[vmem] * 3, out_specs=[vmem] * 2,...  2.01 us

profile of v1, /device:TPU:1, one launch (start us, length us, event | category | flops | bytes accessed | tf_op | source)
XLA Modules:
  0.0 55.7 jit_solution(13607387304496112450)
XLA Ops:
  0.6 53.0 %shard_map.95 = (f32[16,128]{1,0:T(8,128)}, bf16[128,128]{1,0:T(8,128)(2,1)}) custom-call(bf16[1024,1024]{1,0:T(8,128)(2,1)} %bitcast.8, bf16[100,1024]{1,0:T(8,128)(2,1)} %bitcast.9, f32[100,1024]{1,0:T(8,128)} %target_hbm.1, f32[8,128]{1,0:T(8,128)} %bitcast.14, f32[1,100]{1,0:T(1,128)} %bitcast.15, s32[3,1024]{1,0:T(4,128)} %bitcast.11, ...), custom_call_target="tpu_custom_call" | custom-call | tf_op jit(solution)/shard_map/pallas_call | solution.py:409
  53.7 2.0 %shard_map.96 = (f32[16,100]{1,0:T(8,128)}, bf16[128,1024]{1,0:T(8,128)(2,1)}) custom-call(f32[16,128]{1,0:T(8,128)} %get-tuple-element.6.gw_ref, bf16[128,128]{1,0:T(8,128)(2,1)} %get-tuple-element.7.mesh_ref, bf16[100,1024]{1,0:T(8,128)(2,1)} %bitcast.10), custom_call_target="tpu_custom_call" | custom-call | tf_op jit(solution)/shard_map/pallas_call | solution.py:465

commit v2 on v1

--- a/solution.py
+++ b/solution.py
@@ -222,8 +222,7 @@
         wb_s[rows, :] = jnp.dot(sel_s[...], spread, preferred_element_type=jnp.float32)
         return 0
 
-    early = (groups + 1) // 2
-    lax.fori_loop(0, early, one_hot, 0)
+    lax.fori_loop(0, 1, one_hot, 0)
     vcol = jnp.broadcast_to(
         jnp.concatenate([var[...], jnp.zeros((1, LANES - variables), jnp.float32)], axis=1), (LANES, LANES)
     ).T
@@ -261,7 +260,8 @@
         m = lax.rem(e + o, members)
         send(g_send.at[m], g_recv.at[e], g_ss, g_rs, "ens", m, e)
 
-    lax.fori_loop(early, groups, one_hot, 0)
+    early = max(1, groups // 2)
+    lax.fori_loop(1, early, one_hot, 0)
 
     bulk_wait(g_recv, g_rs)
     pad = jnp.zeros((LANES - grows, LANES), jnp.float32)
@@ -280,7 +280,7 @@
                 send(out_buf.at[zs, j], in_buf.at[zs, u], m_ss, m_rs.at[at], "grid", plane_peer(j), g)
         return 0
 
-    lax.fori_loop(0, 1, messages, 0)
+    lax.fori_loop(0, early, messages, 0)
 
     wide = jnp.concatenate([g_recv[s] for s in range(members)], axis=1)
     for b in range(0, latent, 2 * LANES):
@@ -297,7 +297,12 @@
     )
     half.start()
 
-    lax.fori_loop(1, max(1, groups // 2), messages, 0)
+    def late_messages(t, _):
+        one_hot(t, 0)
+        return messages(t, 0)
+
+    middle = (early + groups) // 2
+    lax.fori_loop(early, middle, late_messages, 0)
 
     half.wait_recv()
     total = gw_s[:, core] + half_recv[...]
@@ -307,7 +312,7 @@
         m = lax.rem(e + o, members)
         send(y_send.at[m], y_recv.at[e], y_ss, y_rs, "ens", m, e)
 
-    lax.fori_loop(max(1, groups // 2), groups, messages, 0)
+    lax.fori_loop(middle, groups, late_messages, 0)
 
     pick = (lax.broadcasted_iota(jnp.int32, (16, LANES), 1) == variables).astype(jnp.float32).astype(jnp.bfloat16)
     ids = lax.broadcasted_iota(jnp.int32, (mesh_rows, step), 0).astype(jnp.float32)

time: 56 us -> 56.3 us (level); the launches traced: 55.7 us -> 55.3 us
  no operation moved by 1% of the time
where the time goes in v2:
time: 56.3 us; the launch traced here: 55.3 us
  Pallas kernels  54.7 us (97%)
  between operations  0.64 us (1%)
    pallas_call x1, Pallas kernels, per_device(): pl.pallas_call(functools.partial(fused_kernel, (variables, slots, share,...  52.6 us
    pallas_call x1, Pallas kernels, per_device(): pl.pallas_call(finish_kernel, in_specs=[vmem] * 3, out_specs=[vmem] * 2,...  2.01 us

profile of v2, /device:TPU:1, one launch (start us, length us, event | category | flops | bytes accessed | tf_op | source)
XLA Modules:
  0.0 55.3 jit_solution(1185288928659307605)
XLA Ops:
  0.6 52.6 %shard_map.95 = (f32[16,128]{1,0:T(8,128)}, bf16[128,128]{1,0:T(8,128)(2,1)}) custom-call(bf16[1024,1024]{1,0:T(8,128)(2,1)} %bitcast.8, bf16[100,1024]{1,0:T(8,128)(2,1)} %bitcast.9, f32[100,1024]{1,0:T(8,128)} %target_hbm.1, f32[8,128]{1,0:T(8,128)} %bitcast.14, f32[1,100]{1,0:T(1,128)} %bitcast.15, s32[3,1024]{1,0:T(4,128)} %bitcast.11, ...), custom_call_target="tpu_custom_call" | custom-call | tf_op jit(solution)/shard_map/pallas_call | solution.py:414
  53.3 2.0 %shard_map.96 = (f32[16,100]{1,0:T(8,128)}, bf16[128,1024]{1,0:T(8,128)(2,1)}) custom-call(f32[16,128]{1,0:T(8,128)} %get-tuple-element.6.gw_ref, bf16[128,128]{1,0:T(8,128)(2,1)} %get-tuple-element.7.mesh_ref, bf16[100,1024]{1,0:T(8,128)(2,1)} %bitcast.10), custom_call_target="tpu_custom_call" | custom-call | tf_op jit(solution)/shard_map/pallas_call | solution.py:470

commit v3 on v2

--- a/solution.py
+++ b/solution.py
@@ -3,6 +3,7 @@
 
 import jax
 import jax.numpy as jnp
+import numpy as np
 from jax import lax
 from jax.experimental import pallas as pl
 from jax.experimental.pallas import tpu as pltpu
@@ -77,6 +78,27 @@
         x_s[b : b + LANES, LANES:] = jnp.concatenate([owns, blank], axis=0).T.astype(jnp.bfloat16)
 
 
+def packing(variables, slots, capacity, nu):
+    used = variables + 1
+    width = LANES - used
+    pieces = -(-used // width)
+    keep = round_up(-(-capacity * pieces // (pieces + 1)), 16)
+    late, hosts = slots - keep, keep // pieces
+    assert capacity - keep <= hosts and late <= LANES
+    shift = np.zeros((LANES, pieces * LANES), np.float32)
+    for v in range(used):
+        shift[v, v // width * LANES + used + v % width] = 1
+    grow = np.zeros((nu * keep, pieces * nu * late), np.float32)
+    order = np.zeros((pieces * nu * hosts, nu * keep), np.float32)
+    for o in range(nu):
+        for i in range(hosts):
+            for q in range(pieces):
+                if i < late:
+                    grow[o * keep + pieces * i + q, (q * nu + o) * late + i] = 1
+                order[(q * nu + o) * hosts + i, o * keep + pieces * i + q] = 1
+    return keep, pieces, [a.astype(jnp.bfloat16) for a in (shift, grow, order, shift.T.copy())]
+
+
 def far_first(n):
     return sorted(range(n), key=lambda o: -min(o, n - o))
 
@@ -87,15 +109,17 @@
 
 def fused_kernel(
     cfg,
-    hidden_hbm, wt_hbm, target_hbm, area_hbm, var_hbm, own_hbm, row_hbm, ew_hbm,
+    hidden_hbm, wt_hbm, target_hbm, area_hbm, var_hbm, own_hbm, row_hbm, ew_hbm, plans_hbm,
     gw_out, mesh_out,
-    hid, wt_raw, target, area, var, own, row, ew,
+    hid, wt_raw, target, area, var, own, row, ew, shift_s, grow_s, order_s, back_s,
     wt, w_col, x_send, x_recv, unit_s, g_send, g_recv,
     slot_s, x_s, a_s, sel_s, wb_s, gt_s, out_buf, in_buf,
     d_send, d_recv, gw_s, half_recv, y_send, y_recv, q_s, gq_s, q_recv, p_send, p_recv, r_send, r_recv,
     in_sem, x_ss, x_rs, g_ss, g_rs, m_ss, m_rs, d_ss, d_rs, h_ss, h_rs, y_ss, y_rs, q_ss, q_rs, p_ss, p_rs, r_ss, r_rs,
 ):
-    variables, slots, share, normalizer = cfg
+    variables, slots, share, normalizer, pieces = cfg
+    keep = out_buf.shape[2]
+    late = slots - keep
     members, grows, slab = g_send.shape
     owners, points = slot_s.shape
     latent = hid.shape[1]
@@ -154,6 +178,14 @@
     )
     for i, (s, d) in enumerate(((area_hbm, area), (var_hbm, var), (own_hbm, own), (row_hbm, row), (ew_hbm, ew))):
         loads.append(pltpu.make_async_copy(s, d, in_sem.at[n_hid + 1 + i]))
+    start = 0
+    for ref in (shift_s, grow_s, order_s, back_s):
+        for b in range(0, ref.shape[1], LANES):
+            rows = pl.ds(start, ref.shape[0])
+            loads.append(
+                pltpu.make_async_copy(plans_hbm.at[rows], ref.at[:, pl.ds(b, LANES)], in_sem.at[len(loads)])
+            )
+            start += ref.shape[0]
     for cp in loads:
         cp.start()
     lax.fori_loop(1, members, greet_ens, 0)
@@ -273,14 +305,22 @@
         rows = pl.ds(pl.multiple_of(at * (both * step), both * step), both * step)
         picked = jnp.dot(a_s[rows, :], gt_s[...], preferred_element_type=jnp.float32)
         zs = pl.ds(at * both, both)
-        out_buf[zs] = (picked * wb_s[rows, :]).astype(jnp.bfloat16).reshape(both, nu, slots, LANES)
+        message = picked * wb_s[rows, :]
+        for i in range(both):
+            at_o = [i * step + o * slots for o in range(nu)]
+            head = jnp.concatenate([message[k : k + keep, :] for k in at_o], axis=0)
+            rest = jnp.concatenate([message[k + keep : k + slots, :] for k in at_o], axis=0).astype(jnp.bfloat16)
+            moved = jnp.dot(rest, shift_s[...], preferred_element_type=jnp.float32).astype(jnp.bfloat16)
+            moved = jnp.concatenate([moved[:, q * LANES : (q + 1) * LANES] for q in range(pieces)], axis=0)
+            moved = jnp.dot(grow_s[...], moved, preferred_element_type=jnp.float32)
+            out_buf[at * both + i] = (head + moved).astype(jnp.bfloat16).reshape(nu, keep, LANES)
         for o in far_first(nx):
             for c in range(nc):
                 j = lax.rem(x_at + o, nx) * nc + lax.rem(core + 1 + c, nc)
                 send(out_buf.at[zs, j], in_buf.at[zs, u], m_ss, m_rs.at[at], "grid", plane_peer(j), g)
         return 0
 
-    lax.fori_loop(0, early, messages, 0)
+    lax.fori_loop(0, 1, messages, 0)
 
     wide = jnp.concatenate([g_recv[s] for s in range(members)], axis=1)
     for b in range(0, latent, 2 * LANES):
@@ -301,8 +341,7 @@
         one_hot(t, 0)
         return messages(t, 0)
 
-    middle = (early + groups) // 2
-    lax.fori_loop(early, middle, late_messages, 0)
+    lax.fori_loop(1, early, messages, 0)
 
     half.wait_recv()
     total = gw_s[:, core] + half_recv[...]
@@ -312,10 +351,11 @@
         m = lax.rem(e + o, members)
         send(y_send.at[m], y_recv.at[e], y_ss, y_rs, "ens", m, e)
 
-    lax.fori_loop(middle, groups, late_messages, 0)
+    lax.fori_loop(early, groups, late_messages, 0)
 
     pick = (lax.broadcasted_iota(jnp.int32, (16, LANES), 1) == variables).astype(jnp.float32).astype(jnp.bfloat16)
-    ids = lax.broadcasted_iota(jnp.int32, (mesh_rows, step), 0).astype(jnp.float32)
+    wide_step = round_up(nu * keep + nu * keep // pieces + 1, LANES)
+    ids = lax.broadcasted_iota(jnp.int32, (mesh_rows, wide_step), 0).astype(jnp.float32)
 
     def mesh_part(t, _):
         at = lax.rem(z // both + 1 + t, groups)
@@ -323,7 +363,13 @@
         bulk_wait(in_buf.at[zs], m_rs.at[at])
         for i in range(both):
             zi = at * both + i
-            block = in_buf[zi].reshape(step, LANES)
+            head = in_buf[zi].reshape(nu * keep, LANES)
+            moved = jnp.dot(order_s[...], head, preferred_element_type=jnp.float32).astype(jnp.bfloat16)
+            hosts = nu * keep // pieces
+            moved = jnp.concatenate([moved[q * hosts : (q + 1) * hosts, :] for q in range(pieces)], axis=1)
+            moved = jnp.dot(moved, back_s[...], preferred_element_type=jnp.float32).astype(jnp.bfloat16)
+            empty = jnp.zeros((wide_step - nu * keep - hosts, LANES), jnp.bfloat16)
+            block = jnp.concatenate([head, moved, empty], axis=0)
             place = lax.dot_general(pick, block, (((1,), (1,)), ((), ())), preferred_element_type=jnp.float32)
             picker = jnp.where(place[0:1, :] == ids, 1.0, 0.0).astype(jnp.bfloat16)
             d_send[zi] = jnp.dot(picker, block, preferred_element_type=jnp.float32).astype(jnp.bfloat16)
@@ -405,6 +451,8 @@
     nx, nz, nc = grid_shape(owners)
     nu = nx * nc
     share = latent // (owners * members)
+    keep, pieces, plans = packing(variables, slots, capacity, nu)
+    packed = np.concatenate([a[:, b : b + LANES] for a in plans for b in range(0, a.shape[1], LANES)], axis=0)
     normalizer = 1.0 / math.sqrt(float(points * owners * members))
     f32, bf16, i32 = jnp.float32, jnp.bfloat16, jnp.int32
     hbm = pl.BlockSpec(memory_space=pltpu.HBM)
@@ -412,8 +460,8 @@
     dma = pltpu.SemaphoreType.DMA
     wt = weight.T
     gw, mesh_sum = pl.pallas_call(
-        functools.partial(fused_kernel, (variables, slots, share, normalizer)),
-        in_specs=[hbm] * 8,
+        functools.partial(fused_kernel, (variables, slots, share, normalizer, pieces)),
+        in_specs=[hbm] * 9,
         out_specs=[vmem] * 2,
         out_shape=[
             jax.ShapeDtypeStruct((members * share, LANES), f32),
@@ -428,6 +476,7 @@
             pltpu.VMEM((neigh, points), i32),
             pltpu.VMEM((neigh, points), i32),
             pltpu.VMEM((neigh, points), f32),
+            *[pltpu.VMEM(a.shape, bf16) for a in plans],
             pltpu.VMEM((LANES, latent), bf16),
             pltpu.VMEM((latent, LANES), bf16),
             pltpu.VMEM((members, grows, slab), jnp.int16),
@@ -441,8 +490,8 @@
             pltpu.VMEM((min(2, nz) * nu * slots, LANES), bf16),
             pltpu.VMEM((owners * slots, LANES), f32),
             pltpu.VMEM((points, LANES), bf16),
-            pltpu.VMEM((nz, nu, slots, LANES), bf16),
-            pltpu.VMEM((nz, nu, slots, LANES), bf16),
+            pltpu.VMEM((nz, nu, keep, LANES), bf16),
+            pltpu.VMEM((nz, nu, keep, LANES), bf16),
             pltpu.VMEM((nz, mesh_rows, LANES), bf16),
             pltpu.VMEM((nz, mesh_rows, LANES), bf16),
             pltpu.VMEM((nx * nz, nc, members * share, LANES), f32),
@@ -456,7 +505,7 @@
             pltpu.VMEM((nz, share, LANES), f32),
             pltpu.VMEM((share, LANES), f32),
             pltpu.VMEM((members, share, LANES), f32),
-            dma((7 + points // (2 * slab),)),
+            dma((7 + sum(a.shape[1] // LANES for a in plans) + points // (2 * slab),)),
             dma(()), dma(()), dma(()), dma(()), dma(()), dma((nz,)), dma(()), dma(()),
             dma(()), dma(()), dma(()), dma(()), dma(()), dma(()), dma(()), dma(()), dma(()), dma(()),
         ],
@@ -465,7 +514,7 @@
         ),
     )(
         rows, wt, target, area_weight.reshape(points // LANES, LANES), var_weight.reshape(1, variables),
-        edge_owner.T, edge_row.T, edge_weight.T,
+        edge_owner.T, edge_row.T, edge_weight.T, jnp.asarray(packed),
     )
     grad_weight, mesh_grad = pl.pallas_call(
         finish_kernel,

time: 56.3 us -> 59 us (1.048); the launches traced: 55.3 us -> 58.9 us
  Pallas kernels: 54.7 us -> 58.3 us
    pallas_call x1, Pallas kernels: 52.6 us -> 56.3 us  [per_device(): pl.pallas_call(functools.partial(fused_kernel, (variables, slots, share,...]
where the time goes in v3:
time: 59 us; the launch traced here: 58.9 us
  Pallas kernels  58.3 us (99%)
  between operations  0.64 us (1%)
    pallas_call x1, Pallas kernels, per_device(): pl.pallas_call(functools.partial(fused_kernel, (variables, slots, share,...  56.3 us
    pallas_call x1, Pallas kernels, per_device(): pl.pallas_call(finish_kernel, in_specs=[vmem] * 3, out_specs=[vmem] * 2,...  2 us

profile of v3, /device:TPU:1, one launch (start us, length us, event | category | flops | bytes accessed | tf_op | source)
XLA Modules:
  0.0 58.9 jit_solution(13355267059458138249)
XLA Ops:
  0.6 56.3 %shard_map.104 = (f32[16,128]{1,0:T(8,128)}, bf16[128,128]{1,0:T(8,128)(2,1)}) custom-call(bf16[1024,1024]{1,0:T(8,128)(2,1)} %bitcast.8, bf16[100,1024]{1,0:T(8,128)(2,1)} %bitcast.9, f32[100,1024]{1,0:T(8,128)} %target_hbm.1, f32[8,128]{1,0:T(8,128)} %bitcast.14, f32[1,100]{1,0:T(1,128)} %bitcast.15, s32[3,1024]{1,0:T(4,128)} %bitcast.11, ...), custom_call_target="tpu_custom_call" | custom-call | tf_op jit(solution)/shard_map/pallas_call | solution.py:462
  56.9 2.0 %shard_map.105 = (f32[16,100]{1,0:T(8,128)}, bf16[128,1024]{1,0:T(8,128)(2,1)}) custom-call(f32[16,128]{1,0:T(8,128)} %get-tuple-element.6.gw_ref, bf16[128,128]{1,0:T(8,128)(2,1)} %get-tuple-element.7.mesh_ref, bf16[100,1024]{1,0:T(8,128)(2,1)} %bitcast.10), custom_call_target="tpu_custom_call" | custom-call | tf_op jit(solution)/shard_map/pallas_call | solution.py:519

commit v4 on v2

--- a/solution.py
+++ b/solution.py
@@ -113,6 +113,14 @@
     def column_peer(i):
         return ((u // nc) * nz + i) * nc + lax.rem(u, nc)
 
+    def send_known(src, dst, ss, rs, to, own):
+        if own:
+            pltpu.make_async_copy(src, dst, rs).start()
+        else:
+            pltpu.make_async_remote_copy(
+                src_ref=src, dst_ref=dst, send_sem=ss, recv_sem=rs, device_id=to, device_id_type=pl.DeviceIdType.MESH
+            ).start()
+
     def send(src, dst, ss, rs, axis, peer, me):
         @pl.when(peer != me)
         def _():
@@ -189,7 +197,10 @@
             pl.semaphore_wait(barrier, members + nu + nz - 3)
         for s in range(2):
             m = 2 * c + s
-            send(x_send.at[m], x_recv.at[e], x_ss, x_rs, "ens", m, e)
+            if t < chunks - 1:
+                send_known(x_send.at[m], x_recv.at[e], x_ss, x_rs, (m, g), False)
+            else:
+                send(x_send.at[m], x_recv.at[e], x_ss, x_rs, "ens", m, e)
 
     for cp in loads[n_hid:]:
         cp.wait()
@@ -258,7 +269,7 @@
     )
     for o in far_first(members):
         m = lax.rem(e + o, members)
-        send(g_send.at[m], g_recv.at[e], g_ss, g_rs, "ens", m, e)
+        send_known(g_send.at[m], g_recv.at[e], g_ss, g_rs, (m, g), o == 0)
 
     early = max(1, groups // 2)
     lax.fori_loop(1, early, one_hot, 0)
@@ -276,8 +287,11 @@
         out_buf[zs] = (picked * wb_s[rows, :]).astype(jnp.bfloat16).reshape(both, nu, slots, LANES)
         for o in far_first(nx):
             for c in range(nc):
-                j = lax.rem(x_at + o, nx) * nc + lax.rem(core + 1 + c, nc)
-                send(out_buf.at[zs, j], in_buf.at[zs, u], m_ss, m_rs.at[at], "grid", plane_peer(j), g)
+                x_to, c_to = lax.rem(x_at + o, nx), lax.rem(core + 1 + c, nc)
+                send_known(
+                    out_buf.at[zs, x_to * nc + c_to], in_buf.at[zs, u], m_ss, m_rs.at[at],
+                    (e, (x_to * nz + z) * nc + c_to), o == 0 and c == nc - 1,
+                )
         return 0
 
     lax.fori_loop(0, early, messages, 0)
@@ -310,7 +324,7 @@
         y_send[m] = total[:, m * share : (m + 1) * share, :]
     for o in far_first(members):
         m = lax.rem(e + o, members)
-        send(y_send.at[m], y_recv.at[e], y_ss, y_rs, "ens", m, e)
+        send_known(y_send.at[m], y_recv.at[e], y_ss, y_rs, (m, g), o == 0)
 
     lax.fori_loop(middle, groups, late_messages, 0)
 
@@ -337,8 +351,9 @@
     for m in range(1, members):
         total = total + y_recv[m]
     gq_s[...] = total.reshape(nx, nz, share, LANES)
-    for j in range(nx):
-        send(gq_s.at[j], q_recv.at[x_at], q_ss, q_rs, "grid", plane_peer(j * nc + core), g)
+    for o in far_first(nx):
+        j = lax.rem(x_at + o, nx)
+        send_known(gq_s.at[j], q_recv.at[x_at], q_ss, q_rs, (e, (j * nz + z) * nc + core), o == 0)
 
     lax.fori_loop(groups // 2, groups - 1, mesh_part, 0)
 
@@ -347,15 +362,16 @@
     for j in range(1, nx):
         total = total + q_recv[j]
     p_send[...] = total
-    for j in range(nz):
-        send(p_send.at[j], p_recv.at[z], p_ss, p_rs, "grid", column_peer(j), g)
+    for o in far_first(nz):
+        j = lax.rem(z + o, nz)
+        send_known(p_send.at[j], p_recv.at[z], p_ss, p_rs, (e, (x_at * nz + j) * nc + core), o == 0)
 
     lax.fori_loop(groups - 1, groups, mesh_part, 0)
 
     bulk_wait(p_recv, p_rs)
     r_send[...] = jnp.sum(p_recv[...], axis=0) * normalizer
-    for m in range(members):
-        send(r_send, r_recv.at[e], r_ss, r_rs, "ens", m, e)
+    for o in far_first(members):
+        send_known(r_send, r_recv.at[e], r_ss, r_rs, (lax.rem(e + o, members), g), o == 0)
     bulk_wait(d_recv, d_rs)
     acc = d_recv[0].astype(jnp.float32)
     for j in range(1, nz):

time: 56.3 us -> 56.1 us (level)
  no operation moved by 1% of the time
where the time goes in v4:
time: 56.1 us; the launch traced here: 55.2 us
  Pallas kernels  54.6 us (97%)
  between operations  0.64 us (1%)
    pallas_call x1, Pallas kernels, per_device(): pl.pallas_call(functools.partial(fused_kernel, (variables, slots, share,...  52.6 us
    pallas_call x1, Pallas kernels, per_device(): pl.pallas_call(finish_kernel, in_specs=[vmem] * 3, out_specs=[vmem] * 2,...  2.01 us

profile of v4, /device:TPU:1, one launch (start us, length us, event | category | flops | bytes accessed | tf_op | source)
XLA Modules:
  0.0 55.2 jit_solution(111741258496576214)
XLA Ops:
  0.6 52.6 %shard_map.95 = (f32[16,128]{1,0:T(8,128)}, bf16[128,128]{1,0:T(8,128)(2,1)}) custom-call(bf16[1024,1024]{1,0:T(8,128)(2,1)} %bitcast.8, bf16[100,1024]{1,0:T(8,128)(2,1)} %bitcast.9, f32[100,1024]{1,0:T(8,128)} %target_hbm.1, f32[8,128]{1,0:T(8,128)} %bitcast.14, f32[1,100]{1,0:T(1,128)} %bitcast.15, s32[3,1024]{1,0:T(4,128)} %bitcast.11, ...), custom_call_target="tpu_custom_call" | custom-call | tf_op jit(solution)/shard_map/pallas_call | solution.py:430
  53.2 2.0 %shard_map.96 = (f32[16,100]{1,0:T(8,128)}, bf16[128,1024]{1,0:T(8,128)(2,1)}) custom-call(f32[16,128]{1,0:T(8,128)} %get-tuple-element.6.gw_ref, bf16[128,128]{1,0:T(8,128)(2,1)} %get-tuple-element.7.mesh_ref, bf16[100,1024]{1,0:T(8,128)(2,1)} %bitcast.10), custom_call_target="tpu_custom_call" | custom-call | tf_op jit(solution)/shard_map/pallas_call | solution.py:486
